TPU v7x, 256 devices: a whole 4x4x8 slice. The times are simulated.
256 devices in a mesh: row: 16 (over z, y_hi), col: 16 (over y_lo, x, core).
Axes of the slice: x: 4, y: 4 (y_hi: 2, y_lo: 2; y = y_hi * 2 + y_lo), z: 8, core: 2. Of those that a mesh axis runs over, the one named last changes fastest.
Arguments:
- basis_values: bfloat16 [4, 8192, 16384], P(None, 'row', 'col'), may hold values from -6 to 6
- density: float32 [8192, 2560], P('row'), may hold values from -1 to 1, as said below
- screen: int32 [64, 128], P('row', 'col'), may hold values 0 or 1
- atom_of_block: int32 [128], P('col'), may hold values from 0 to 63
- atom_factor: float32 [64], replicated, may hold values from 0.5 to 2
- quad_weight: float32 [16384], P('col'), may hold values from 0.5 to 2
- core_density: float32 [16384], P('col'), may hold values from 0.3 to 1
Outputs:
- xc_matrix: float32 [8192, 1536], P(('row', 'col'))
Inputs may be any that keep to these rules, and one draw needn't show every extreme that they name: The density matrix is symmetric. Column block k of a row (k from 0 to 4, 512 columns each) holds the row's entries with the basis block k - 2 places further along the closed chain of 16 blocks; all other entries are zero.
All inputs are finite; a program needn't handle non-finite values. No bound on the sum of `screen` on one device may be relied on, other than what follows from the above.
Results may differ from a plain program's by a relative error of at most 0.0014.
Values may be sent and summed in bfloat16 or wider, within the bound.
A program may use at most 64 MiB of HBM per device.

v0:
```python
import math

import jax
import jax.numpy as jnp
from jax import lax
from jax.sharding import PartitionSpec as P

BAND = 5


KAPPA_VALUE = 0.804
MU_VALUE = 0.22
SLATER_COEF = 0.7386


def from_behind(block, axis, distance):
    devices = range(lax.axis_size(axis))
    route = [((i - distance) % len(devices), i) for i in devices]
    return lax.ppermute(block, axis, route)


def energy_density(density_in, squared_in, core):
    regular = jnp.sqrt(density_in * density_in + core * core)
    reduced = squared_in * regular ** (-8.0 / 3.0)
    enhance = 1.0 + KAPPA_VALUE - KAPPA_VALUE / (1.0 + MU_VALUE * reduced / KAPPA_VALUE)
    return -SLATER_COEF * regular ** (4.0 / 3.0) * enhance


def potentials(density_in, squared_in, core):

    def total_energy(first_arg, second_arg):
        return jnp.sum(energy_density(first_arg, second_arg, core))

    return jax.grad(total_energy, argnums=(0, 1))(density_in, squared_in)


def masked_basis(basis_values, screen):
    components, row_count, points = basis_values.shape
    row_blocks, point_blocks = screen.shape
    shaped = basis_values.reshape(
        components, row_blocks, row_count // row_blocks, point_blocks, points // point_blocks
    )
    keeper = screen.astype(basis_values.dtype)[None, :, None, :, None]
    return (shaped * keeper).reshape(components, row_count, points)


def contract(left_side, right_side):
    return lax.dot_general(
        left_side, right_side, (((1,), (1,)), ((), ())), preferred_element_type=jnp.float32
    )


def body(basis_values, density, screen, atom_of_block, atom_factor, quad_weight, core_density):
    masked = masked_basis(basis_values, screen)
    values = masked[0]
    row_count, points = values.shape
    reach = BAND // 2
    nearby = {0: values}
    for heading in (1, -1):
        current = values
        for stride in range(1, reach + 1):
            current = from_behind(current, "row", -heading)
            nearby[heading * stride] = current
    applied = jnp.zeros((row_count, points), jnp.float32)
    for offset in range(-reach, reach + 1):
        column = offset + reach
        strip = density[:, column * row_count : (column + 1) * row_count]
        applied = applied + jnp.dot(
            strip, nearby[offset].astype(jnp.float32), precision=lax.Precision.HIGHEST
        )
    masked32 = masked.astype(jnp.float32)
    partial_sums = jnp.einsum("cmg,mg->cg", masked32, applied, precision=lax.Precision.HIGHEST)
    summed = lax.psum(partial_sums, "row")
    point_density = summed[0]
    gradient = 2.0 * summed[1:]
    squared = jnp.sum(gradient * gradient, axis=0)
    atoms = atom_factor.shape[0]
    chooser = (atom_of_block[:, None] == jnp.arange(atoms, dtype=jnp.int32)[None, :]).astype(
        jnp.float32
    )
    block_factor = jnp.dot(chooser, atom_factor, precision=lax.Precision.HIGHEST)
    group_size = points // atom_of_block.shape[0]
    weights = (quad_weight.reshape(-1, group_size) * block_factor[:, None]).reshape(
        points
    ) / math.sqrt(points * lax.axis_size("col"))
    density_pot, gradient_pot = potentials(point_density, squared, core_density)
    scalar_part = 0.5 * weights * density_pot
    vector_part = 2.0 * weights * gradient_pot * gradient
    half_pot = (
        scalar_part * masked32[0] + jnp.sum(vector_part[:, None, :] * masked32[1:], axis=0)
    ).astype(jnp.bfloat16)
    further = {0: half_pot}
    for offset in range(1, reach + 1):
        further[offset] = from_behind(half_pot, "row", -offset)
    pieces = []
    for offset in range(reach + 1):
        pieces.append(contract(half_pot, nearby[offset]) + contract(values, further[offset]))
    return lax.psum_scatter(jnp.concatenate(pieces, axis=1), "col", scatter_dimension=0, tiled=True)


def solution(mesh):
    in_specs = (
        P(None, "row", "col"),
        P("row", None),
        P("row", "col"),
        P("col"),
        P(),
        P("col"),
        P("col"),
    )
    out_specs = P(("row", "col"), None)
    return jax.shard_map(body, mesh=mesh, in_specs=in_specs, out_specs=out_specs, check_vma=False)
```

profile of v0, /device:TPU:1, one launch (start us, length us, event | category | flops | bytes accessed | tf_op | source)
XLA Modules:
  0.0 313.2 jit_solution(7516777395357345013)
XLA Ops:
  6.5 0.0 copy-start
  6.5 0.0 reduce-scatter.4.cloned.1.call-start
  6.5 0.7 convert_element_type.21
  7.2 3.3 %copy.21 = bf16[256,8,8,128]{3,2,1,0:T(8,128)(2,1)S(1)} copy(bf16[256,8,8,128]{3,1,2,0:T(8,128)(2,1)} %bitcast.65) | data formatting | bytes 8388608
  10.5 0.1 slice_multiply_fusion.1
  10.7 0.0 copy-start.1
  10.7 0.3 copy.32
  10.9 3.8 %collective-permute-start = (bf16[512,1024]{1,0:T(8,128)(2,1)S(1)}, bf16[512,1024]{1,0:T(8,128)(2,1)S(1)}, u32[]{:S(2)}, u32[]{:S(2)}) collective-permute-start(bf16[512,1024]{1,0:T(8,128)(2,1)S(1)} %bitcast.78), channel_id=1, source_target_pairs={{240,0},{0,16},{16,32},{32,48},{48,64},{64,80},{80,96},{96,112},{1... | collective-permute-start | bytes 3145736 | tf_op jit(solution)/shard_map/ppermute | solution.py:19
  14.8 5.4 %collective-permute-start.2 = (bf16[512,1024]{1,0:T(8,128)(2,1)S(1)}, bf16[512,1024]{1,0:T(8,128)(2,1)S(1)}, u32[]{:S(2)}, u32[]{:S(2)}) collective-permute-start(bf16[512,1024]{1,0:T(8,128)(2,1)S(1)} %bitcast.79), channel_id=1, source_target_pairs={{16,0},{32,16},{48,32},{64,48},{80,64},{96,80},{112,96},{128,112},... | collective-permute-start | bytes 3145736 | tf_op jit(solution)/shard_map/ppermute | solution.py:19
  20.1 0.2 mul.148
  20.4 0.0 slice-start
  20.4 0.3 copy.31
  20.6 0.0 copy-done.1
  20.7 0.0 slice-start.1
  20.7 4.2 %multiply_convert_fusion = f32[4,512,1024]{2,1,0:T(8,128)} fusion(bf16[4,512,1024]{2,1,0:T(8,128)(2,1)S(1)} %copy-done.1, bf16[512,1024]{1,0:T(8,128)(2,1)S(1)} %bitcast.72), kind=kLoop, calls=%fused_computation.3 | loop fusion | flops 4194304 | bytes 13631488 | tf_op jit(solution)/shard_map/convert_element_type | solution.py:71
  24.9 0.0 copy-start.6
  24.9 34.2 %collective-permute-done = bf16[512,1024]{1,0:T(8,128)(2,1)S(1)} collective-permute-done((bf16[512,1024]{1,0:T(8,128)(2,1)S(1)}, bf16[512,1024]{1,0:T(8,128)(2,1)S(1)}, u32[]{:S(2)}, u32[]{:S(2)}) %collective-permute-start) | collective-permute-done | bytes 1048608 | tf_op jit(solution)/shard_map/ppermute | solution.py:19
  59.1 3.7 %collective-permute-start.1 = (bf16[512,1024]{1,0:T(8,128)(2,1)S(1)}, bf16[512,1024]{1,0:T(8,128)(2,1)S(1)}, u32[]{:S(2)}, u32[]{:S(2)}) collective-permute-start(bf16[512,1024]{1,0:T(8,128)(2,1)S(1)} %collective-permute-done), channel_id=1, source_target_pairs={{240,0},{0,16},{16,32},{32,48},{48,64},{64,80},{80,96},{96,112},{1... | collective-permute-start | bytes 3145736 | tf_op jit(solution)/shard_map/ppermute | solution.py:19
  62.8 0.0 slice-done
  62.8 0.0 slice-done.1
  62.8 2.2 fusion.8
  65.0 0.0 collective-permute-done.2
  65.0 0.0 copy-start.2
  65.0 5.6 %collective-permute-start.3 = (bf16[512,1024]{1,0:T(8,128)(2,1)S(1)}, bf16[512,1024]{1,0:T(8,128)(2,1)S(1)}, u32[]{:S(2)}, u32[]{:S(2)}) collective-permute-start(bf16[512,1024]{1,0:T(8,128)(2,1)S(1)} %collective-permute-done.2), channel_id=1, source_target_pairs={{16,0},{32,16},{48,32},{64,48},{80,64},{96,80},{112,96},{128,112},... | collective-permute-start | bytes 3145736 | tf_op jit(solution)/shard_map/ppermute | solution.py:19
  70.6 0.0 copy-done
  70.6 0.0 copy-done.6
  70.6 0.2 convolution_bitcast_fusion
  70.8 2.2 fusion.10
  73.0 2.2 fusion.6
  75.2 0.0 copy-done.2
  75.2 31.0 %collective-permute-done.1 = bf16[512,1024]{1,0:T(8,128)(2,1)S(1)} collective-permute-done((bf16[512,1024]{1,0:T(8,128)(2,1)S(1)}, bf16[512,1024]{1,0:T(8,128)(2,1)S(1)}, u32[]{:S(2)}, u32[]{:S(2)}) %collective-permute-start.1) | collective-permute-done | bytes 1048608 | tf_op jit(solution)/shard_map/ppermute | solution.py:19
  106.1 2.2 fusion.12
  108.4 5.8 %collective-permute-done.3 = bf16[512,1024]{1,0:T(8,128)(2,1)S(1)} collective-permute-done((bf16[512,1024]{1,0:T(8,128)(2,1)S(1)}, bf16[512,1024]{1,0:T(8,128)(2,1)S(1)}, u32[]{:S(2)}, u32[]{:S(2)}) %collective-permute-start.3) | collective-permute-done | bytes 1048608 | tf_op jit(solution)/shard_map/ppermute | solution.py:19
  114.2 3.9 %add_add_fusion = f32[1024,512]{1,0:T(8,128)} fusion(f32[1024,512]{1,0:T(8,128)S(1)} %fusion.6, f32[1024,512]{1,0:T(8,128)S(1)} %fusion.8, f32[1024,512]{1,0:T(8,128)S(1)} %fusion.12, f32[1024,512]{1,0:T(8,128)S(1)} %fusion.10, bf16[512,1024]{1,0:T(8,128)(2,1)S(1)} %collective-permute-done.3, f32[512,2560]{1,0:T(8,128)S(1)} %bitcast.76), kind=kOutput, calls=%fused_computation.10 | convolution fusion | flops 3223322624 | bytes 12582912 | tf_op jit(solution)/shard_map/dot_general | solution.py:68
  118.1 2.9 copy.19
  121.0 0.0 copy-start.4
  121.0 0.0 copy-start.5
  121.0 4.3 %multiply_reduce_fusion = f32[1024,4]{0,1:T(4,128)S(1)} fusion(f32[1024,512]{0,1:T(8,128)} %copy.19, bf16[4,512,1024]{2,1,0:T(8,128)(2,1)} %param.7, bf16[512,1024]{1,0:T(8,128)(2,1)S(1)} %bitcast.73), kind=kLoop, calls=%fused_computation | loop fusion | flops 8384512 | bytes 7356416 | tf_op jit(solution)/shard_map/cmg,mg->cg/dot_general | solution.py:72
  125.3 61.1 %psum.7 = f32[4,1024]{1,0:T(4,128)S(1)} all-reduce(f32[4,1024]{1,0:T(4,128)S(1)} %bitcast.80), channel_id=1, replica_groups=mesh['row'=16,'col'=16] {'row'}, use_global_device_ids=true, to_apply=%region_0.0 | all-reduce | flops 4096 | bytes 32768 | tf_op jit(solution)/shard_map/psum | solution.py:73
  186.4 0.0 copy-done.4
  186.4 0.0 copy-done.5
  186.4 0.1 multiply_multiply_fusion
  186.5 3.9 %fusion = f32[512,1024]{1,0:T(8,128)S(1)} fusion(f32[4,512,1024]{2,1,0:T(8,128)} %multiply_convert_fusion, f32[3,1024]{1,0:T(4,128)S(1)} %slice_multiply_fusion.2), kind=kLoop, calls=%fused_computation.2 | loop fusion | flops 2621440 | bytes 8400896 | tf_op jit(solution)/shard_map/reduce_sum | solution.py:90
  190.4 1.9 fusion.2
  192.3 0.1 collective-permute-start.5
  192.4 0.1 collective-permute-start.4
  192.5 1.9 fusion.4
  194.4 0.7 fusion.18
  195.1 0.7 convolution_add_fusion.2
  195.9 10.1 %collective-permute-done.5 = bf16[512,1024]{1,0:T(8,128)(2,1)S(1)} collective-permute-done((bf16[512,1024]{1,0:T(8,128)(2,1)S(1)}, bf16[512,1024]{1,0:T(8,128)(2,1)S(1)}, u32[]{:S(2)}, u32[]{:S(2)}) %collective-permute-start.5) | collective-permute-done | bytes 1048608 | tf_op jit(solution)/shard_map/ppermute | solution.py:19
  206.0 0.7 fusion.16
  206.8 0.0 copy-start.3
  206.8 0.7 convolution_add_fusion
  207.6 13.2 %collective-permute-done.4 = bf16[512,1024]{1,0:T(8,128)(2,1)S(1)} collective-permute-done((bf16[512,1024]{1,0:T(8,128)(2,1)S(1)}, bf16[512,1024]{1,0:T(8,128)(2,1)S(1)}, u32[]{:S(2)}, u32[]{:S(2)}) %collective-permute-start.4) | collective-permute-done | bytes 1048608 | tf_op jit(solution)/shard_map/ppermute | solution.py:19
  220.8 0.7 fusion.17
  221.5 0.0 copy-done.3
  221.6 0.8 convolution_add_fusion.1
  222.3 0.3 pad_maximum_fusion
  222.6 2.3 copy.17
  225.0 0.0 reduce-scatter.4.cloned.1.call-update
  225.0 81.3 %reduce-scatter.4.cloned.1.call-done = f32[32,1536]{1,0:T(8,128)} async-done(((f32[512,1536]{1,0:T(8,128)}), f32[32,1536]{1,0:T(8,128)}) %reduce-scatter.4.cloned.1.call-update) | async-done | bytes 196624 | tf_op jit(solution)/shard_map/reduce_scatter | solution.py:98
  (4 shorter events, 0.0 us)
Async XLA Ops:
  6.5 64.0 %copy-start = (f32[64]{0:T(128)S(1)}, f32[64]{0:T(128)}, u32[]{:S(2)}) copy-start(f32[64]{0:T(128)} %param.11) | copy-start | bytes 772
  6.5 299.8 %reduce-scatter.4.cloned.1.call-start = ((), (), s32[]{:S(2)}) async-start(), calls=%async_computation.1 | async-start | bytes 3342336 | tf_op jit(solution)/shard_map/reduce_scatter | solution.py:98
  10.7 10.0 %copy-start.1 = (bf16[4,512,1024]{2,1,0:T(8,128)(2,1)S(1)}, bf16[4,512,1024]{2,1,0:T(8,128)(2,1)}, u32[]{:S(2)}) copy-start(bf16[4,512,1024]{2,1,0:T(8,128)(2,1)} %param.7) | copy-start | bytes 12582916
  10.9 48.1 %collective-permute-start = (bf16[512,1024]{1,0:T(8,128)(2,1)S(1)}, bf16[512,1024]{1,0:T(8,128)(2,1)S(1)}, u32[]{:S(2)}, u32[]{:S(2)}) collective-permute-start(bf16[512,1024]{1,0:T(8,128)(2,1)S(1)} %bitcast.78), channel_id=1, source_target_pairs={{240,0},{0,16},{16,32},{32,48},{48,64},{64,80},{80,96},{96,112},{1... | collective-permute-start | bytes 3145736 | tf_op jit(solution)/shard_map/ppermute | solution.py:19
  14.8 50.2 %collective-permute-start.2 = (bf16[512,1024]{1,0:T(8,128)(2,1)S(1)}, bf16[512,1024]{1,0:T(8,128)(2,1)S(1)}, u32[]{:S(2)}, u32[]{:S(2)}) collective-permute-start(bf16[512,1024]{1,0:T(8,128)(2,1)S(1)} %bitcast.79), channel_id=1, source_target_pairs={{16,0},{32,16},{48,32},{64,48},{80,64},{96,80},{112,96},{128,112},... | collective-permute-start | bytes 3145736 | tf_op jit(solution)/shard_map/ppermute | solution.py:19
  20.4 42.4 %slice-start = ((s8[5242880]{0:T(1024)(128)(4,1)}), s8[4194304]{0:T(1024)(128)(4,1)S(1)}, s32[]{:S(2)}) async-start(s8[5242880]{0:T(1024)(128)(4,1)} %bitcast.75), calls=%async_computation.2 | async-start | bytes 8388608
  20.7 42.1 %slice-start.1 = ((s8[5242880]{0:T(1024)(128)(4,1)}), s8[1048576]{0:T(1024)(128)(4,1)S(1)}, s32[]{:S(2)}) async-start(s8[5242880]{0:T(1024)(128)(4,1)} %bitcast.75), calls=%async_computation.3 | async-start | bytes 2097152
  24.9 45.7 %copy-start.6 = (s32[8]{0:T(128)S(1)}, s32[8]{0:T(128)}, u32[]{:S(2)}) copy-start(s32[8]{0:T(128)} %param.10) | copy-start | bytes 100
  59.1 47.1 %collective-permute-start.1 = (bf16[512,1024]{1,0:T(8,128)(2,1)S(1)}, bf16[512,1024]{1,0:T(8,128)(2,1)S(1)}, u32[]{:S(2)}, u32[]{:S(2)}) collective-permute-start(bf16[512,1024]{1,0:T(8,128)(2,1)S(1)} %collective-permute-done), channel_id=1, source_target_pairs={{240,0},{0,16},{16,32},{32,48},{48,64},{64,80},{80,96},{96,112},{1... | collective-permute-start | bytes 3145736 | tf_op jit(solution)/shard_map/ppermute | solution.py:19
  65.0 10.2 %copy-start.2 = (bf16[512,1024]{1,0:T(8,128)(2,1)}, bf16[512,1024]{1,0:T(8,128)(2,1)S(1)}, u32[]{:S(2)}) copy-start(bf16[512,1024]{1,0:T(8,128)(2,1)S(1)} %collective-permute-done.2) | copy-start | bytes 3145732
  65.0 49.1 %collective-permute-start.3 = (bf16[512,1024]{1,0:T(8,128)(2,1)S(1)}, bf16[512,1024]{1,0:T(8,128)(2,1)S(1)}, u32[]{:S(2)}, u32[]{:S(2)}) collective-permute-start(bf16[512,1024]{1,0:T(8,128)(2,1)S(1)} %collective-permute-done.2), channel_id=1, source_target_pairs={{16,0},{32,16},{48,32},{64,48},{80,64},{96,80},{112,96},{128,112},... | collective-permute-start | bytes 3145736 | tf_op jit(solution)/shard_map/ppermute | solution.py:19
  121.0 65.4 %copy-start.4 = (f32[1024]{0:T(1024)S(1)}, f32[1024]{0:T(1024)}, u32[]{:S(2)}) copy-start(f32[1024]{0:T(1024)} %param.12) | copy-start | bytes 12292
  121.0 65.4 %copy-start.5 = (f32[1024]{0:T(1024)S(1)}, f32[1024]{0:T(1024)}, u32[]{:S(2)}) copy-start(f32[1024]{0:T(1024)} %param.13) | copy-start | bytes 12292
  192.3 13.7 %collective-permute-start.5 = (bf16[512,1024]{1,0:T(8,128)(2,1)S(1)}, bf16[512,1024]{1,0:T(8,128)(2,1)S(1)}, u32[]{:S(2)}, u32[]{:S(2)}) collective-permute-start(bf16[512,1024]{1,0:T(8,128)(2,1)S(1)} %fusion.2), channel_id=1, source_target_pairs={{32,0},{48,16},{64,32},{80,48},{96,64},{112,80},{128,96},{144,112}... | collective-permute-start | bytes 3145736 | tf_op jit(solution)/shard_map/ppermute | solution.py:19
  192.4 28.4 %collective-permute-start.4 = (bf16[512,1024]{1,0:T(8,128)(2,1)S(1)}, bf16[512,1024]{1,0:T(8,128)(2,1)S(1)}, u32[]{:S(2)}, u32[]{:S(2)}) collective-permute-start(bf16[512,1024]{1,0:T(8,128)(2,1)S(1)} %fusion.2), channel_id=1, source_target_pairs={{16,0},{32,16},{48,32},{64,48},{80,64},{96,80},{112,96},{128,112},... | collective-permute-start | bytes 3145736 | tf_op jit(solution)/shard_map/ppermute | solution.py:19
  206.8 14.8 %copy-start.3 = (bf16[512,1024]{1,0:T(8,128)(2,1)S(1)}, bf16[512,1024]{1,0:T(8,128)(2,1)}, u32[]{:S(2)}) copy-start(bf16[512,1024]{1,0:T(8,128)(2,1)} %copy-done.2) | copy-start | bytes 3145732
Sparse Core Ops, SparseCore 0:
  225.1 81.1 reduce-scatter.3
where the time goes:
time: 316 us; the launch traced here: 313 us
  waiting for transfers between devices  176 us (56%)
  blocking collectives  61.1 us (19%)
  starting transfers between devices  18.6 us (6%)
  other arithmetic  17.5 us (6%)
  matrix products  17.4 us (6%)
  between operations  13.7 us (4%)
  local copies, waits for them, and re-layouts  9.31 us (3%)
    ppermute x6, waiting for transfers between devices, from_behind(): return lax.ppermute(block, axis, route)  94.3 us
    reduce_scatter x1, waiting for transfers between devices, body(): lax.psum_scatter(jnp.concatenate(pieces, axis=1), 'col', scatter_dimensio...  81.3 us
    psum x1, blocking collectives, body(): summed = lax.psum(partial_sums, 'row')  61.1 us
    ppermute x6, starting transfers between devices, from_behind(): return lax.ppermute(block, axis, route)  18.6 us
    dot_general x5, matrix products, body(): jnp.dot(strip, nearby[offset].astype(jnp.float32), precision=lax.Precisio...  12.7 us
    unnamed x23, local copies, waits for them, and re-layouts  9.1 us
  transfers between devices with their start and end apart: 7, of which 6 were waited for; matrix products, arithmetic and copies ran while one was open for 6% of the time, Pallas kernels for 0%

commit v1 on v0

v1 whole, which is shorter than its diff:
```python
import functools
import math

import jax
import jax.numpy as jnp
from jax import lax
from jax.experimental import pallas as pl
from jax.experimental.pallas import tpu as pltpu
from jax.sharding import PartitionSpec as P

F32, BF16 = jnp.float32, jnp.bfloat16
MESH = pl.DeviceIdType.MESH
BAND = 5
KAPPA_VALUE = 0.804
MU_VALUE = 0.22
SLATER_COEF = 0.7386

TILE = 128
CHUNK = 256
X_CHIPS, Y_LOW, CORES, PLANES = 4, 2, 2, 8


def potentials(point, squared, core):
    t_square = point * point + core * core
    log_t = 0.5 * jnp.log(t_square)
    reduced = squared * jnp.exp((-8.0 / 3.0) * log_t)
    inverse = 1.0 / (1.0 + (MU_VALUE / KAPPA_VALUE) * reduced)
    enhance = 1.0 + KAPPA_VALUE - KAPPA_VALUE * inverse
    slope = MU_VALUE * inverse * inverse
    slope_reduced = MU_VALUE * (reduced * inverse) * inverse
    along_t = -SLATER_COEF * jnp.exp((1.0 / 3.0) * log_t) * ((4.0 / 3.0) * enhance - (8.0 / 3.0) * slope_reduced)
    density_pot = along_t * (point * jnp.exp(-log_t))
    gradient_pot = -SLATER_COEF * slope * jnp.exp((-4.0 / 3.0) * log_t)
    return density_pot, gradient_pot


def kernel(
    basis, dens, screen, atom, factor, quad, core_dens, out,
    raw0, comps, dens32, dens_cat, phi, applied, half, acc, part_a, part_b, sum_a, coef,
    core_recv, send_a, send_b, own_a, own_b, recv_a, recv_b, fin, fin_recv,
    raw_sem, comp_sem, dens_sem, phi_send, phi_recv, pa_send, pa_recv, pb_send, pb_recv,
    c_send, c_recv, ra_send, ra_recv, rb_send, rb_recv, f_send, f_recv,
):
    rows = basis.shape[1]
    points = basis.shape[2]
    steps = points // CHUNK
    blocks = CHUNK // TILE
    row_tiles = rows // TILE
    row, col = lax.axis_index("row"), lax.axis_index("col")
    plane, side = row // 2, row % 2
    low, chip_x, core = col // (X_CHIPS * CORES), (col // CORES) % X_CHIPS, col % CORES
    way = 1 - 2 * side

    def at_row(new_plane, new_side):
        return {"row": lax.rem(new_plane + PLANES, PLANES) * 2 + new_side, "col": col}

    def at_chip(dy, dx):
        return {"row": row, "col": (((low + dy) % Y_LOW) * X_CHIPS + (chip_x + dx) % X_CHIPS) * CORES + core}

    paired = plane + 1 - 2 * (plane % 2)
    partner = at_row(plane, 1 - side)
    far, near = at_row(plane + way, side), at_row(plane - way, side)
    odd = at_row(plane - way, 1 - side)
    group_a = [partner, at_row(paired, side), at_row(paired, 1 - side)]
    group_b = [at_row(plane + 2, side), at_row(plane + 4, side), at_row(plane + 6, side)]
    sibling = {"row": row, "col": col + 1 - 2 * core}
    chips = [(dy, dx) for dy in range(Y_LOW) for dx in range(X_CHIPS) if dy or dx]
    chip_ids = [at_chip(dy, dx) for dy, dx in chips]
    behind1 = {"row": lax.rem(row + 15, 16), "col": col}
    behind2 = {"row": lax.rem(row + 14, 16), "col": col}

    def raw_copy(j):
        return pltpu.make_async_copy(basis.at[0, :, pl.ds(j * CHUNK, CHUNK)], raw0.at[j], raw_sem.at[j])

    def comp_copy(j):
        return pltpu.make_async_copy(basis.at[pl.ds(1, 3), :, pl.ds(j * CHUNK, CHUNK)], comps.at[j], comp_sem.at[j])

    dens_copy = pltpu.make_async_copy(dens, dens32, dens_sem)
    for j in range(steps):
        raw_copy(j).start()
    dens_copy.start()
    for j in range(steps):
        comp_copy(j).start()

    barrier = pltpu.get_barrier_semaphore()
    peers = [partner, far, near, odd, group_a[2], *group_b, sibling, *chip_ids]
    for peer in peers:
        pl.semaphore_signal(barrier, inc=1, device_id=peer, device_id_type=MESH)

    def remote(src, dst, send, recv, device):
        return pltpu.make_async_remote_copy(
            src_ref=src, dst_ref=dst, send_sem=send, recv_sem=recv, device_id=device, device_id_type=MESH
        )

    def own_sends(j):
        return [
            remote(phi.at[j, 2], phi.at[j, 2 - way], phi_send.at[0, j], phi_recv.at[0, j], partner),
            remote(phi.at[j, 2], phi.at[j, 2 - 2 * way], phi_send.at[1, j], phi_recv.at[1, j], far),
            remote(phi.at[j, 2], phi.at[j, 2 + 2 * way], phi_send.at[2, j], phi_recv.at[2, j], near),
        ]

    def own_recvs(j):
        return [
            remote(phi.at[j, 2], phi.at[j, 2 + way], phi_send.at[0, j], phi_recv.at[0, j], partner),
            remote(phi.at[j, 2], phi.at[j, 2 - 2 * way], phi_send.at[1, j], phi_recv.at[1, j], near),
            remote(phi.at[j, 2], phi.at[j, 2 + 2 * way], phi_send.at[2, j], phi_recv.at[2, j], far),
        ]

    def forward(j):
        even = j % 2 == 0
        src = jnp.where(even, 2 + way, 2 + 2 * way)
        dst = jnp.where(even, 2 - way, 2 + way)
        target = {"row": jnp.where(even, far["row"], partner["row"]), "col": col}
        return remote(phi.at[j, src], phi.at[j, dst], phi_send.at[3, j], phi_recv.at[3, j], target)

    def forward_recv(j):
        return remote(phi.at[j, 2], phi.at[j, 2 - way], phi_send.at[3, j], phi_recv.at[3, j], partner)

    def keep(i, j, b):
        return screen[i, j * blocks + b].astype(F32)

    def tile(i, b):
        return slice(i * TILE, (i + 1) * TILE), slice(b * TILE, (b + 1) * TILE)

    def mask_own(j):
        for i in range(row_tiles):
            for b in range(blocks):
                r, c = tile(i, b)
                phi[j, 2, r, c] = (raw0[j, r, c].astype(F32) * keep(i, j, b)).astype(BF16)

    raw_copy(0).wait()
    mask_own(0)
    pl.semaphore_wait(barrier, len(peers))
    for copy in own_sends(0):
        copy.start()
    for j in range(1, steps):
        raw_copy(j).wait()
        mask_own(j)
        if j == 1:
            for copy in own_sends(1):
                copy.start()

    dens_copy.wait()

    @pl.loop(0, rows // 32)
    def _(i):
        at = pl.multiple_of(i * 32, 32)
        whole = dens32[pl.ds(at, 32), :]
        high = whole.astype(BF16)
        dens_cat[pl.ds(at, 32), :] = high
        dens_cat[pl.ds(rows + at, 32), :] = (whole - high.astype(F32)).astype(BF16)

    acc[...] = jnp.zeros_like(acc)

    def a_copies(j):
        return [
            remote(part_a.at[j, 3], part_a.at[j, i], pa_send.at[j, i], pa_recv.at[j, i], peer)
            for i, peer in enumerate(group_a)
        ]

    def b_copies(j):
        return [
            remote(sum_a.at[j], part_b.at[j, i], pb_send.at[j, i], pb_recv.at[j, i], peer)
            for i, peer in enumerate(group_b)
        ]

    def density_step(j):
        applied[...] = jnp.dot(
            dens_cat[...], phi[j].reshape(BAND * rows, CHUNK), preferred_element_type=F32
        )
        for b in range(blocks):
            sums = [jnp.zeros((1, TILE), F32)] * 4
            for i in range(row_tiles):
                r, c = tile(i, b)
                low_rows = slice(rows + i * TILE, rows + (i + 1) * TILE)
                mine = (applied[r, c] + applied[low_rows, c]) * keep(i, j, b)
                sums[0] = sums[0] + jnp.sum(mine * phi[j, 2, r, c].astype(F32), axis=0, keepdims=True)
                for d in range(3):
                    sums[d + 1] = sums[d + 1] + jnp.sum(mine * comps[j, d, r, c].astype(F32), axis=0, keepdims=True)
            for d in range(4):
                part_a[j, 3, d * blocks + b : d * blocks + b + 1, :] = sums[d]

    def potential_step(j):
        total = sum_a[j]
        for i in range(3):
            total = total + part_b[j, i]
        point = total[0:blocks]
        grads = [2.0 * total[d * blocks : (d + 1) * blocks] for d in (1, 2, 3)]
        squared = grads[0] * grads[0] + grads[1] * grads[1] + grads[2] * grads[2]
        at = j * blocks
        lines = [quad[pl.ds(at + b, 1), :] * factor[atom[at + b]] for b in range(blocks)]
        weights = jnp.concatenate(lines, axis=0) * (1.0 / math.sqrt(points * 16))
        density_pot, gradient_pot = potentials(point, squared, core_dens[pl.ds(at, blocks), :])
        coef[0:blocks, :] = 0.5 * weights * density_pot
        for d in range(3):
            coef[(d + 1) * blocks : (d + 2) * blocks, :] = 2.0 * weights * gradient_pot * grads[d]
        for b in range(blocks):
            factors = [coef[d * blocks + b : d * blocks + b + 1, :] for d in range(4)]
            for i in range(row_tiles):
                r, c = tile(i, b)
                value = factors[0] * phi[j, 2, r, c].astype(F32)
                rest = factors[1] * comps[j, 0, r, c].astype(F32)
                for d in range(1, 3):
                    rest = rest + factors[d + 1] * comps[j, d, r, c].astype(F32)
                half[r, c] = ((value + rest) * keep(i, j, b)).astype(BF16)

    def matrix_step(j):
        def contract(left, right):
            return lax.dot_general(left, right, (((1,), (1,)), ((), ())), preferred_element_type=F32)

        shape = acc.shape[1:]
        pot = half[...]
        acc[0] += contract(phi[j, 0], pot).reshape(shape)
        acc[1] += contract(phi[j, 1], pot).reshape(shape)
        acc[2] += (contract(pot, phi[j, 2]) + contract(phi[j, 2], pot)).reshape(shape)
        acc[3] += contract(pot, phi[j, 3]).reshape(shape)
        acc[4] += contract(pot, phi[j, 4]).reshape(shape)

    def wait_direct(j):
        partner_in, near_in, far_in = own_recvs(j)
        partner_in.wait_recv()
        far_in.wait_recv()

    wait_direct(0)
    forward(0).start()

    @pl.loop(0, steps + 1)
    def _(t):
        @pl.when(t + 1 < steps)
        def _():
            wait_direct(t + 1)
            forward(t + 1).start()

        @pl.when(t + 2 < steps)
        def _():
            for copy in own_sends(t + 2):
                copy.start()

        @pl.when(t >= 1)
        def _():
            j = t - 1
            for copy in a_copies(j):
                copy.wait_recv()
            sum_a[j] = (part_a[j, 3] + part_a[j, 0]) + (part_a[j, 1] + part_a[j, 2])
            for copy in b_copies(j):
                copy.start()

        @pl.when(t < steps)
        def _():
            own_recvs(t)[1].wait_recv()
            forward_recv(t).wait_recv()
            comp_copy(t).wait()
            density_step(t)
            for copy in a_copies(t):
                copy.start()

        @pl.when(t >= 1)
        def _():
            j = t - 1
            for copy in b_copies(j):
                copy.wait_recv()
            potential_step(j)
            matrix_step(j)

    def core_copy(k):
        return remote(acc.at[k, :, 1 - core], core_recv.at[k], c_send.at[k], c_recv.at[k], sibling)

    for k in range(BAND):
        core_copy(k).start()
    mine = low * X_CHIPS + chip_x

    def fold(k, send, own, place):
        core_copy(k).wait_recv()
        total = acc[k, :, core] + core_recv[k]
        acc[k, :, core] = total
        send[:, place] = total.astype(BF16)
        own[place] = acc[k, mine, core]

    def chip_copies(send, recv, ssem, rsem):
        return [
            remote(send.at[((low + dy) % Y_LOW) * X_CHIPS + (chip_x + dx) % X_CHIPS], recv.at[i], ssem.at[i], rsem.at[i], peer)
            for i, ((dy, dx), peer) in enumerate(zip(chips, chip_ids))
        ]

    fold(0, send_a, own_a, 0)
    fold(1, send_a, own_a, 1)
    copies_a = chip_copies(send_a, recv_a, ra_send, ra_recv)
    for copy in copies_a:
        copy.start()
    for k in (2, 3, 4):
        fold(k, send_b, own_b, k - 2)
    copies_b = chip_copies(send_b, recv_b, rb_send, rb_recv)
    for copy in copies_b:
        copy.start()

    for copy in copies_a:
        copy.wait_recv()
    total = own_a[...]
    for i in range(len(chips)):
        total = total + recv_a[i].astype(F32)
    fin[...] = total
    last = [
        remote(fin.at[0], fin_recv.at[0], f_send.at[0], f_recv.at[0], behind2),
        remote(fin.at[1], fin_recv.at[1], f_send.at[1], f_recv.at[1], behind1),
    ]
    for copy in last:
        copy.start()
    for copy in copies_b:
        copy.wait_recv()
    for k in range(3):
        total = own_b[k]
        for i in range(len(chips)):
            total = total + recv_b[i, k].astype(F32)
        if k:
            last[2 - k].wait_recv()
            total = total + fin_recv[2 - k]
        out[:, k * rows : (k + 1) * rows] = total

    for j in range(steps):
        for copy in own_sends(j):
            copy.wait_send()
        forward(j).wait_send()
        for copy in a_copies(j) + b_copies(j):
            copy.wait_send()
    for k in range(BAND):
        core_copy(k).wait_send()
    for copy in copies_a + copies_b + last:
        copy.wait_send()


def body(basis_values, density, screen, atom_of_block, atom_factor, quad_weight, core_density):
    rows, points = basis_values.shape[1:]
    steps = points // CHUNK
    piece = rows // 16
    dma = pltpu.SemaphoreType.DMA
    vmem, smem, hbm = (pl.BlockSpec(memory_space=s) for s in (pltpu.VMEM, pltpu.SMEM, pl.ANY))
    flat = 4 * CHUNK // TILE
    return pl.pallas_call(
        kernel,
        out_shape=jax.ShapeDtypeStruct((piece, 3 * rows), F32),
        in_specs=[hbm, hbm, smem, smem, smem, vmem, vmem],
        out_specs=vmem,
        scratch_shapes=[
            pltpu.VMEM((steps, rows, CHUNK), BF16),
            pltpu.VMEM((steps, 3, rows, CHUNK), BF16),
            pltpu.VMEM((rows, BAND * rows), F32),
            pltpu.VMEM((2 * rows, BAND * rows), BF16),
            pltpu.VMEM((steps, BAND, rows, CHUNK), BF16),
            pltpu.VMEM((2 * rows, CHUNK), F32),
            pltpu.VMEM((rows, CHUNK), BF16),
            pltpu.VMEM((BAND, 8, CORES, piece, rows), F32),
            pltpu.VMEM((steps, 4, flat, TILE), F32),
            pltpu.VMEM((steps, 3, flat, TILE), F32),
            pltpu.VMEM((steps, flat, TILE), F32),
            pltpu.VMEM((flat, TILE), F32),
            pltpu.VMEM((BAND, 8, piece, rows), F32),
            pltpu.VMEM((8, 2, piece, rows), BF16),
            pltpu.VMEM((8, 3, piece, rows), BF16),
            pltpu.VMEM((2, piece, rows), F32),
            pltpu.VMEM((3, piece, rows), F32),
            pltpu.VMEM((7, 2, piece, rows), BF16),
            pltpu.VMEM((7, 3, piece, rows), BF16),
            pltpu.VMEM((2, piece, rows), F32),
            pltpu.VMEM((2, piece, rows), F32),
            dma((steps,)), dma((steps,)), dma,
            dma((4, steps)), dma((4, steps)),
            dma((steps, 3)), dma((steps, 3)), dma((steps, 3)), dma((steps, 3)),
            dma((BAND,)), dma((BAND,)),
            dma((7,)), dma((7,)), dma((7,)), dma((7,)),
            dma((2,)), dma((2,)),
        ],
        compiler_params=pltpu.CompilerParams(
            collective_id=0, has_side_effects=True, vmem_limit_bytes=56 << 20
        ),
        name="xc_matrix",
    )(
        basis_values, density, screen, atom_of_block, atom_factor,
        quad_weight.reshape(-1, TILE), core_density.reshape(-1, TILE),
    )


def solution(mesh):
    in_specs = (
        P(None, "row", "col"),
        P("row", None),
        P("row", "col"),
        P("col"),
        P(),
        P("col"),
        P("col"),
    )
    out_specs = P(("row", "col"), None)
    return jax.shard_map(body, mesh=mesh, in_specs=in_specs, out_specs=out_specs, check_vma=False)
```

time: 316 us -> 94.1 us (0.30)
  waiting for transfers between devices: 176 us -> 0 us
  Pallas kernels: 0 us -> 92.3 us
  blocking collectives: 61.1 us -> 0 us
  starting transfers between devices: 18.6 us -> 0 us
  other arithmetic: 17.5 us -> 0 us
  matrix products: 17.4 us -> 0 us
  between operations: 13.7 us -> 0.01 us
  local copies, waits for them, and re-layouts: 9.31 us -> 1.62 us
    ppermute x6 -> x0, waiting for transfers between devices: 94.3 us -> none  [from_behind(): return lax.ppermute(block, axis, route)]
    pallas_call x0 -> x1, Pallas kernels: none -> 92.3 us  [body(): pl.pallas_call(kernel, out_shape=jax.ShapeDtypeStruct((piece, 3 * rows),...]
    reduce_scatter x1 -> x0, waiting for transfers between devices: 81.3 us -> none  [body(): lax.psum_scatter(jnp.concatenate(pieces, axis=1), 'col', scatter_dimensio...]
    psum x1 -> x0, blocking collectives: 61.1 us -> none  [body(): summed = lax.psum(partial_sums, 'row')]
    ppermute x6 -> x0, starting transfers between devices: 18.6 us -> none  [from_behind(): return lax.ppermute(block, axis, route)]
    dot_general x12 -> x0, matrix products: 17.4 us -> none  [the longest x5 12.7 us: body(): jnp.dot(strip, nearby[offset].astype(jnp.float32), precision=lax.Precisio...]
    convert_element_type x4 -> x0, other arithmetic: 8.68 us -> none  [the longest x1 4.19 us: body(): masked32 = masked.astype(jnp.float32)]
    unnamed x23 -> x1, local copies, waits for them, and re-layouts: 9.1 us -> 1.62 us
  transfers between devices with their start and end apart: 7 -> 0, of which waited for: 6 -> 0; matrix products, arithmetic and copies ran while one was open for 6% -> 0% of each run, Pallas kernels for 0% -> 0%
where the time goes in v1:
time: 94.1 us; the launch traced here: 94 us
  Pallas kernels  92.3 us (98%)
  local copies, waits for them, and re-layouts  1.62 us (2%)
    pallas_call x1, Pallas kernels, body(): pl.pallas_call(kernel, out_shape=jax.ShapeDtypeStruct((piece, 3 * rows),...  92.3 us

profile of v1, /device:TPU:1, one launch (start us, length us, event | category | flops | bytes accessed | tf_op | source)
XLA Modules:
  0.0 94.0 jit_solution(1239848024574187952)
XLA Ops:
  0.0 92.3 %xc_matrix.1 = f32[32,1536]{1,0:T(8,128)} custom-call(bf16[4,512,1024]{2,1,0:T(8,128)(2,1)} %basis.1, f32[512,2560]{1,0:T(8,128)} %dens.1, s32[4,8]{1,0:T(4,128)} %screen.1, s32[8]{0:T(128)} %atom.1, f32[64]{0:T(128)} %factor.1, f32[8,128]{1,0:T(8,128)} %bitcast.2, f32[8,128]{1,0:T(8,128)} %bitcast.3), custom_call_target="tpu_custom_call" | custom-call | tf_op jit(solution)/shard_map/xc_matrix/pallas_call | solution.py:338
  92.3 1.6 %copy.9 = f32[32,1536]{1,0:T(8,128)} copy(f32[32,1536]{1,0:T(8,128)} %xc_matrix.1) | data formatting | bytes 393216

commit v2 on v1

--- a/solution.py
+++ b/solution.py
@@ -18,6 +18,9 @@
 TILE = 128
 CHUNK = 256
 X_CHIPS, Y_LOW, CORES, PLANES = 4, 2, 2, 8
+DEPTH = 3
+LEAD = 1
+LAG_A, LAG_B = 1, 2
 
 
 def potentials(point, squared, core):
@@ -36,10 +39,10 @@
 
 def kernel(
     basis, dens, screen, atom, factor, quad, core_dens, out,
-    raw0, comps, dens32, dens_cat, phi, applied, half, acc, part_a, part_b, sum_a, coef,
-    core_recv, send_a, send_b, own_a, own_b, recv_a, recv_b, fin, fin_recv,
+    raw0, comps, dens32, dens_cat, phi, phi_sib, applied, half, half_sib, acc, part_a, part_b, sum_a, coef,
+    send, own, recv, fin, fin_recv,
     raw_sem, comp_sem, dens_sem, phi_send, phi_recv, pa_send, pa_recv, pb_send, pb_recv,
-    c_send, c_recv, ra_send, ra_recv, rb_send, rb_recv, f_send, f_recv,
+    c_send, c_recv, r_send, r_recv, f_send, f_recv,
 ):
     rows = basis.shape[1]
     points = basis.shape[2]
@@ -92,41 +95,51 @@
             src_ref=src, dst_ref=dst, send_sem=send, recv_sem=recv, device_id=device, device_id_type=MESH
         )
 
+    def half_block(j, k, h):
+        return phi.at[j, k, pl.ds(4 * h, 4)]
+
+    def block_copy(j, route, src, dst, h, device):
+        return remote(
+            half_block(j, src, h), half_block(j, dst, h), phi_send.at[route, h, j], phi_recv.at[route, h, j], device
+        )
+
     def own_sends(j):
+        order = [(0, 0), (1, 1), (2, 0), (0, 1), (1, 0), (2, 1)]
+        place = [(2 - way, partner), (2 - 2 * way, far), (2 + 2 * way, near)]
+        return [block_copy(j, route, 2, place[route][0], h, place[route][1]) for route, h in order]
+
+    def block_recv(j, route, h):
+        place = [(2 + way, partner), (2 - 2 * way, near), (2 + 2 * way, far), (2 - way, partner)]
+        return block_copy(j, route, 2, place[route][0], h, place[route][1])
+
+    def forwards(j):
         return [
-            remote(phi.at[j, 2], phi.at[j, 2 - way], phi_send.at[0, j], phi_recv.at[0, j], partner),
-            remote(phi.at[j, 2], phi.at[j, 2 - 2 * way], phi_send.at[1, j], phi_recv.at[1, j], far),
-            remote(phi.at[j, 2], phi.at[j, 2 + 2 * way], phi_send.at[2, j], phi_recv.at[2, j], near),
+            block_copy(j, 3, 2 + way, 2 - way, 0, far),
+            block_copy(j, 3, 2 + 2 * way, 2 + way, 1, partner),
         ]
-
-    def own_recvs(j):
-        return [
-            remote(phi.at[j, 2], phi.at[j, 2 + way], phi_send.at[0, j], phi_recv.at[0, j], partner),
-            remote(phi.at[j, 2], phi.at[j, 2 - 2 * way], phi_send.at[1, j], phi_recv.at[1, j], near),
-            remote(phi.at[j, 2], phi.at[j, 2 + 2 * way], phi_send.at[2, j], phi_recv.at[2, j], far),
-        ]
-
-    def forward(j):
-        even = j % 2 == 0
-        src = jnp.where(even, 2 + way, 2 + 2 * way)
-        dst = jnp.where(even, 2 - way, 2 + way)
-        target = {"row": jnp.where(even, far["row"], partner["row"]), "col": col}
-        return remote(phi.at[j, src], phi.at[j, dst], phi_send.at[3, j], phi_recv.at[3, j], target)
-
-    def forward_recv(j):
-        return remote(phi.at[j, 2], phi.at[j, 2 - way], phi_send.at[3, j], phi_recv.at[3, j], partner)
 
     def keep(i, j, b):
         return screen[i, j * blocks + b].astype(F32)
 
     def tile(i, b):
         return slice(i * TILE, (i + 1) * TILE), slice(b * TILE, (b + 1) * TILE)
+
+    piece = rows // (8 * CORES)
+    tile_shape = (TILE // (CORES * piece), CORES, piece, TILE)
+
+    def folded(i, b):
+        wide = tile_shape[0]
+        return slice(i * wide, (i + 1) * wide), slice(None), slice(None), slice(b * TILE, (b + 1) * TILE)
+
+    def phi_tile(j, i, b):
+        return phi[(j, 2, *folded(i, b))].reshape(TILE, TILE).astype(F32)
 
     def mask_own(j):
         for i in range(row_tiles):
             for b in range(blocks):
                 r, c = tile(i, b)
-                phi[j, 2, r, c] = (raw0[j, r, c].astype(F32) * keep(i, j, b)).astype(BF16)
+                value = (raw0[j, r, c].astype(F32) * keep(i, j, b)).astype(BF16)
+                phi[(j, 2, *folded(i, b))] = value.reshape(tile_shape)
 
     raw_copy(0).wait()
     mask_own(0)
@@ -136,8 +149,8 @@
     for j in range(1, steps):
         raw_copy(j).wait()
         mask_own(j)
-        if j == 1:
-            for copy in own_sends(1):
+        if j < DEPTH:
+            for copy in own_sends(j):
                 copy.start()
 
     dens_copy.wait()
@@ -174,7 +187,7 @@
                 r, c = tile(i, b)
                 low_rows = slice(rows + i * TILE, rows + (i + 1) * TILE)
                 mine = (applied[r, c] + applied[low_rows, c]) * keep(i, j, b)
-                sums[0] = sums[0] + jnp.sum(mine * phi[j, 2, r, c].astype(F32), axis=0, keepdims=True)
+                sums[0] = sums[0] + jnp.sum(mine * phi_tile(j, i, b), axis=0, keepdims=True)
                 for d in range(3):
                     sums[d + 1] = sums[d + 1] + jnp.sum(mine * comps[j, d, r, c].astype(F32), axis=0, keepdims=True)
             for d in range(4):
@@ -198,133 +211,147 @@
             factors = [coef[d * blocks + b : d * blocks + b + 1, :] for d in range(4)]
             for i in range(row_tiles):
                 r, c = tile(i, b)
-                value = factors[0] * phi[j, 2, r, c].astype(F32)
+                value = factors[0] * phi_tile(j, i, b)
                 rest = factors[1] * comps[j, 0, r, c].astype(F32)
                 for d in range(1, 3):
                     rest = rest + factors[d + 1] * comps[j, d, r, c].astype(F32)
-                half[r, c] = ((value + rest) * keep(i, j, b)).astype(BF16)
-
-    def matrix_step(j):
+                pot = ((value + rest) * keep(i, j, b)).astype(BF16)
+                half[(j, *folded(i, b))] = pot.reshape(tile_shape)
+
+    def sibling_blocks(j):
+        ahead, other = pl.ds(2, 3), 1 - core
+        return [
+            remote(phi.at[j, ahead], phi_sib.at[j, ahead], c_send.at[0, j], c_recv.at[0, j], sibling),
+            remote(
+                phi.at[j, pl.ds(0, 2), :, other], phi_sib.at[j, pl.ds(0, 2), :, other],
+                c_send.at[1, j], c_recv.at[1, j], sibling,
+            ),
+        ]
+
+    def sibling_half(j):
+        return remote(half.at[j], half_sib.at[j], c_send.at[2, j], c_recv.at[2, j], sibling)
+
+    def matrix_part(j, block, pot, offsets):
         def contract(left, right):
             return lax.dot_general(left, right, (((1,), (1,)), ((), ())), preferred_element_type=F32)
 
-        shape = acc.shape[1:]
-        pot = half[...]
-        acc[0] += contract(phi[j, 0], pot).reshape(shape)
-        acc[1] += contract(phi[j, 1], pot).reshape(shape)
-        acc[2] += (contract(pot, phi[j, 2]) + contract(phi[j, 2], pot)).reshape(shape)
-        acc[3] += contract(pot, phi[j, 3]).reshape(shape)
-        acc[4] += contract(pot, phi[j, 4]).reshape(shape)
-
-    def wait_direct(j):
-        partner_in, near_in, far_in = own_recvs(j)
-        partner_in.wait_recv()
-        far_in.wait_recv()
-
-    wait_direct(0)
-    forward(0).start()
-
-    @pl.loop(0, steps + 1)
+        own_pot = pot[j, :, core].reshape(rows // CORES, CHUNK)
+        all_pot = pot[j].reshape(rows, CHUNK)
+        for k in offsets:
+            term = 0.0
+            if k <= 2:
+                term = contract(block[j, k, :, core].reshape(rows // CORES, CHUNK), all_pot)
+            if k >= 2:
+                term = term + contract(own_pot, block[j, k].reshape(rows, CHUNK))
+            acc[k] += term.reshape(acc.shape[1:])
+
+    def pass_on(j):
+        first, second = forwards(j)
+        block_recv(j, 0, 0).wait_recv()
+        first.start()
+        block_recv(j, 2, 1).wait_recv()
+        second.start()
+
+    for j in range(LEAD):
+        pass_on(j)
+
+    @pl.loop(0, steps + LAG_B)
     def _(t):
-        @pl.when(t + 1 < steps)
-        def _():
-            wait_direct(t + 1)
-            forward(t + 1).start()
-
-        @pl.when(t + 2 < steps)
-        def _():
-            for copy in own_sends(t + 2):
+        @pl.when(t + DEPTH < steps)
+        def _():
+            for copy in own_sends(t + DEPTH):
                 copy.start()
 
-        @pl.when(t >= 1)
-        def _():
-            j = t - 1
+        @pl.when(t + LEAD < steps)
+        def _():
+            pass_on(t + LEAD)
+
+        @pl.when(t < steps)
+        def _():
+            for route, h in ((0, 1), (2, 0), (1, 0), (1, 1), (3, 0), (3, 1)):
+                block_recv(t, route, h).wait_recv()
+            for copy in sibling_blocks(t):
+                copy.start()
+            comp_copy(t).wait()
+            density_step(t)
+            for copy in a_copies(t):
+                copy.start()
+
+        @pl.when((t >= LAG_A) & (t < steps + LAG_A))
+        def _():
+            j = t - LAG_A
             for copy in a_copies(j):
                 copy.wait_recv()
             sum_a[j] = (part_a[j, 3] + part_a[j, 0]) + (part_a[j, 1] + part_a[j, 2])
             for copy in b_copies(j):
                 copy.start()
 
-        @pl.when(t < steps)
-        def _():
-            own_recvs(t)[1].wait_recv()
-            forward_recv(t).wait_recv()
-            comp_copy(t).wait()
-            density_step(t)
-            for copy in a_copies(t):
-                copy.start()
-
-        @pl.when(t >= 1)
-        def _():
-            j = t - 1
+        @pl.when(t >= LAG_B)
+        def _():
+            j = t - LAG_B
             for copy in b_copies(j):
                 copy.wait_recv()
             potential_step(j)
-            matrix_step(j)
-
-    def core_copy(k):
-        return remote(acc.at[k, :, 1 - core], core_recv.at[k], c_send.at[k], c_recv.at[k], sibling)
-
-    for k in range(BAND):
-        core_copy(k).start()
+            sibling_half(j).start()
+            matrix_part(j, phi, half, range(BAND))
+
+        @pl.when(t >= LAG_B + 1)
+        def _():
+            j = t - LAG_B - 1
+            for copy in (*sibling_blocks(j), sibling_half(j)):
+                copy.wait_recv()
+            matrix_part(j, phi_sib, half_sib, range(BAND))
+
     mine = low * X_CHIPS + chip_x
 
-    def fold(k, send, own, place):
-        core_copy(k).wait_recv()
-        total = acc[k, :, core] + core_recv[k]
-        acc[k, :, core] = total
-        send[:, place] = total.astype(BF16)
-        own[place] = acc[k, mine, core]
-
-    def chip_copies(send, recv, ssem, rsem):
+    def chip_copies(k):
         return [
-            remote(send.at[((low + dy) % Y_LOW) * X_CHIPS + (chip_x + dx) % X_CHIPS], recv.at[i], ssem.at[i], rsem.at[i], peer)
+            remote(
+                send.at[k, ((low + dy) % Y_LOW) * X_CHIPS + (chip_x + dx) % X_CHIPS], recv.at[k, i],
+                r_send.at[k, i], r_recv.at[k, i], peer,
+            )
             for i, ((dy, dx), peer) in enumerate(zip(chips, chip_ids))
         ]
 
-    fold(0, send_a, own_a, 0)
-    fold(1, send_a, own_a, 1)
-    copies_a = chip_copies(send_a, recv_a, ra_send, ra_recv)
-    for copy in copies_a:
-        copy.start()
-    for k in (2, 3, 4):
-        fold(k, send_b, own_b, k - 2)
-    copies_b = chip_copies(send_b, recv_b, rb_send, rb_recv)
-    for copy in copies_b:
-        copy.start()
-
-    for copy in copies_a:
+    for copy in (*sibling_blocks(steps - 1), sibling_half(steps - 1)):
         copy.wait_recv()
-    total = own_a[...]
-    for i in range(len(chips)):
-        total = total + recv_a[i].astype(F32)
-    fin[...] = total
+    for k in range(BAND):
+        matrix_part(steps - 1, phi_sib, half_sib, (k,))
+        send[k] = acc[k].astype(BF16)
+        for copy in chip_copies(k):
+            copy.start()
+        own[k] = acc[k, mine]
+
+    def collect(k):
+        for copy in chip_copies(k):
+            copy.wait_recv()
+        total = own[k]
+        for i in range(len(chips)):
+            total = total + recv[k, i].astype(F32)
+        return total
+
     last = [
         remote(fin.at[0], fin_recv.at[0], f_send.at[0], f_recv.at[0], behind2),
         remote(fin.at[1], fin_recv.at[1], f_send.at[1], f_recv.at[1], behind1),
     ]
-    for copy in last:
-        copy.start()
-    for copy in copies_b:
-        copy.wait_recv()
-    for k in range(3):
-        total = own_b[k]
-        for i in range(len(chips)):
-            total = total + recv_b[i, k].astype(F32)
-        if k:
-            last[2 - k].wait_recv()
-            total = total + fin_recv[2 - k]
-        out[:, k * rows : (k + 1) * rows] = total
+    for k in range(2):
+        fin[k] = collect(k)
+        last[k].start()
+    totals = [collect(k) for k in (2, 3, 4)]
+    out[:, 0:rows] = totals[0]
+    for k in (1, 2):
+        last[2 - k].wait_recv()
+        out[:, k * rows : (k + 1) * rows] = totals[k] + fin_recv[2 - k]
 
     for j in range(steps):
-        for copy in own_sends(j):
+        for copy in (*own_sends(j), *forwards(j)):
             copy.wait_send()
-        forward(j).wait_send()
-        for copy in a_copies(j) + b_copies(j):
+        for copy in (*a_copies(j), *b_copies(j), *sibling_blocks(j), sibling_half(j)):
             copy.wait_send()
     for k in range(BAND):
-        core_copy(k).wait_send()
-    for copy in copies_a + copies_b + last:
+        for copy in chip_copies(k):
+            copy.wait_send()
+    for copy in last:
         copy.wait_send()
 
 
@@ -345,28 +372,26 @@
             pltpu.VMEM((steps, 3, rows, CHUNK), BF16),
             pltpu.VMEM((rows, BAND * rows), F32),
             pltpu.VMEM((2 * rows, BAND * rows), BF16),
-            pltpu.VMEM((steps, BAND, rows, CHUNK), BF16),
+            pltpu.VMEM((steps, BAND, 8, CORES, piece, CHUNK), BF16),
+            pltpu.VMEM((steps, BAND, 8, CORES, piece, CHUNK), BF16),
             pltpu.VMEM((2 * rows, CHUNK), F32),
-            pltpu.VMEM((rows, CHUNK), BF16),
-            pltpu.VMEM((BAND, 8, CORES, piece, rows), F32),
+            pltpu.VMEM((steps, 8, CORES, piece, CHUNK), BF16),
+            pltpu.VMEM((steps, 8, CORES, piece, CHUNK), BF16),
+            pltpu.VMEM((BAND, 8, piece, rows), F32),
             pltpu.VMEM((steps, 4, flat, TILE), F32),
             pltpu.VMEM((steps, 3, flat, TILE), F32),
             pltpu.VMEM((steps, flat, TILE), F32),
             pltpu.VMEM((flat, TILE), F32),
-            pltpu.VMEM((BAND, 8, piece, rows), F32),
-            pltpu.VMEM((8, 2, piece, rows), BF16),
-            pltpu.VMEM((8, 3, piece, rows), BF16),
-            pltpu.VMEM((2, piece, rows), F32),
-            pltpu.VMEM((3, piece, rows), F32),
-            pltpu.VMEM((7, 2, piece, rows), BF16),
-            pltpu.VMEM((7, 3, piece, rows), BF16),
+            pltpu.VMEM((BAND, 8, piece, rows), BF16),
+            pltpu.VMEM((BAND, piece, rows), F32),
+            pltpu.VMEM((BAND, 7, piece, rows), BF16),
             pltpu.VMEM((2, piece, rows), F32),
             pltpu.VMEM((2, piece, rows), F32),
             dma((steps,)), dma((steps,)), dma,
-            dma((4, steps)), dma((4, steps)),
+            dma((4, 2, steps)), dma((4, 2, steps)),
             dma((steps, 3)), dma((steps, 3)), dma((steps, 3)), dma((steps, 3)),
-            dma((BAND,)), dma((BAND,)),
-            dma((7,)), dma((7,)), dma((7,)), dma((7,)),
+            dma((3, steps)), dma((3, steps)),
+            dma((BAND, 7)), dma((BAND, 7)),
             dma((2,)), dma((2,)),
         ],
         compiler_params=pltpu.CompilerParams(

time: 94.1 us -> 83.4 us (0.89)
  Pallas kernels: 92.3 us -> 81.7 us
    pallas_call x1, Pallas kernels: 92.3 us -> 81.7 us  [body(): pl.pallas_call(kernel, out_shape=jax.ShapeDtypeStruct((piece, 3 * rows),...]
where the time goes in v2:
time: 83.4 us; the launch traced here: 83.3 us
  Pallas kernels  81.7 us (98%)
  local copies, waits for them, and re-layouts  1.62 us (2%)
    pallas_call x1, Pallas kernels, body(): pl.pallas_call(kernel, out_shape=jax.ShapeDtypeStruct((piece, 3 * rows),...  81.7 us

profile of v2, /device:TPU:1, one launch (start us, length us, event | category | flops | bytes accessed | tf_op | source)
XLA Modules:
  0.0 83.3 jit_solution(10557673111772151931)
XLA Ops:
  0.0 81.7 %xc_matrix.1 = f32[32,1536]{1,0:T(8,128)} custom-call(bf16[4,512,1024]{2,1,0:T(8,128)(2,1)} %basis.1, f32[512,2560]{1,0:T(8,128)} %dens.1, s32[4,8]{1,0:T(4,128)} %screen.1, s32[8]{0:T(128)} %atom.1, f32[64]{0:T(128)} %factor.1, f32[8,128]{1,0:T(8,128)} %bitcast.2, f32[8,128]{1,0:T(8,128)} %bitcast.3), custom_call_target="tpu_custom_call" | custom-call | tf_op jit(solution)/shard_map/xc_matrix/pallas_call | solution.py:365
  81.7 1.6 %copy.9 = f32[32,1536]{1,0:T(8,128)} copy(f32[32,1536]{1,0:T(8,128)} %xc_matrix.1) | data formatting | bytes 393216

commit v3 on v2

--- a/solution.py
+++ b/solution.py
@@ -17,6 +17,7 @@
 
 TILE = 128
 CHUNK = 256
+X_FIRST = (0, 2, 4)
 X_CHIPS, Y_LOW, CORES, PLANES = 4, 2, 2, 8
 DEPTH = 3
 LEAD = 1
@@ -40,9 +41,9 @@
 def kernel(
     basis, dens, screen, atom, factor, quad, core_dens, out,
     raw0, comps, dens32, dens_cat, phi, phi_sib, applied, half, half_sib, acc, part_a, part_b, sum_a, coef,
-    send, own, recv, fin, fin_recv,
+    send, recv_x, recv_y, mid_y, mid_y32, mid_x, got_y, got_y32, got_x, got_x1, own, fin, fin_recv,
     raw_sem, comp_sem, dens_sem, phi_send, phi_recv, pa_send, pa_recv, pb_send, pb_recv,
-    c_send, c_recv, r_send, r_recv, f_send, f_recv,
+    c_send, c_recv, r_send, r_recv, m_send, m_recv,
 ):
     rows = basis.shape[1]
     points = basis.shape[2]
@@ -57,8 +58,8 @@
     def at_row(new_plane, new_side):
         return {"row": lax.rem(new_plane + PLANES, PLANES) * 2 + new_side, "col": col}
 
-    def at_chip(dy, dx):
-        return {"row": row, "col": (((low + dy) % Y_LOW) * X_CHIPS + (chip_x + dx) % X_CHIPS) * CORES + core}
+    def at_chip(dy, dx, offset=0):
+        return {"row": lax.rem(row + offset + 16, 16), "col": (((low + dy) % Y_LOW) * X_CHIPS + (chip_x + dx) % X_CHIPS) * CORES + core}
 
     paired = plane + 1 - 2 * (plane % 2)
     partner = at_row(plane, 1 - side)
@@ -67,10 +68,10 @@
     group_a = [partner, at_row(paired, side), at_row(paired, 1 - side)]
     group_b = [at_row(plane + 2, side), at_row(plane + 4, side), at_row(plane + 6, side)]
     sibling = {"row": row, "col": col + 1 - 2 * core}
-    chips = [(dy, dx) for dy in range(Y_LOW) for dx in range(X_CHIPS) if dy or dx]
-    chip_ids = [at_chip(dy, dx) for dy, dx in chips]
-    behind1 = {"row": lax.rem(row + 15, 16), "col": col}
-    behind2 = {"row": lax.rem(row + 14, 16), "col": col}
+    across_y = at_chip(1, 0)
+    along_x = [at_chip(0, dx) for dx in range(1, X_CHIPS)]
+    shifted = [at_chip(1, 0, offset) for offset in (-2, 2)]
+    shifted += [at_chip(0, dx, offset) for offset in (-1, 1) for dx in range(1, X_CHIPS)]
 
     def raw_copy(j):
         return pltpu.make_async_copy(basis.at[0, :, pl.ds(j * CHUNK, CHUNK)], raw0.at[j], raw_sem.at[j])
@@ -86,7 +87,7 @@
         comp_copy(j).start()
 
     barrier = pltpu.get_barrier_semaphore()
-    peers = [partner, far, near, odd, group_a[2], *group_b, sibling, *chip_ids]
+    peers = [partner, far, near, odd, group_a[2], *group_b, sibling, across_y, *along_x, *shifted]
     for peer in peers:
         pl.semaphore_signal(barrier, inc=1, device_id=peer, device_id_type=MESH)
 
@@ -302,15 +303,38 @@
                 copy.wait_recv()
             matrix_part(j, phi_sib, half_sib, range(BAND))
 
-    mine = low * X_CHIPS + chip_x
-
-    def chip_copies(k):
+    def first_copies(k):
+        if k in X_FIRST:
+            return [
+                remote(
+                    send.at[k, :, (chip_x + dx + 1) % X_CHIPS], recv_x.at[k, dx], r_send.at[k, dx], r_recv.at[k, dx], peer
+                )
+                for dx, peer in enumerate(along_x)
+            ]
+        return [remote(send.at[k, 1 - low], recv_y.at[k], r_send.at[k, 0], r_recv.at[k, 0], across_y)]
+
+    def second_copies(k):
+        if k == 0:
+            return [
+                remote(mid_y.at[k], got_y.at[k], m_send.at[k, 0], m_recv.at[k, 0], at_chip(1, 0, -2)),
+                remote(fin, fin_recv, m_send.at[k, 1], m_recv.at[k, 1], at_chip(0, 0, -2)),
+            ]
+        if k == 1:
+            return [
+                remote(
+                    mid_x.at[k, (chip_x + dx) % X_CHIPS], got_x1.at[dx], m_send.at[k, dx], m_recv.at[k, dx],
+                    at_chip(0, dx, -1),
+                )
+                for dx in range(X_CHIPS)
+            ]
+        if k in X_FIRST:
+            src, dst = (mid_y32, got_y32) if k == 2 else (mid_y.at[k], got_y.at[k])
+            return [remote(src, dst, m_send.at[k, 0], m_recv.at[k, 0], across_y)]
         return [
             remote(
-                send.at[k, ((low + dy) % Y_LOW) * X_CHIPS + (chip_x + dx) % X_CHIPS], recv.at[k, i],
-                r_send.at[k, i], r_recv.at[k, i], peer,
+                mid_x.at[k, (chip_x + dx + 1) % X_CHIPS], got_x.at[k, dx], m_send.at[k, dx], m_recv.at[k, dx], peer
             )
-            for i, ((dy, dx), peer) in enumerate(zip(chips, chip_ids))
+            for dx, peer in enumerate(along_x)
         ]
 
     for copy in (*sibling_blocks(steps - 1), sibling_half(steps - 1)):
@@ -318,30 +342,55 @@
     for k in range(BAND):
         matrix_part(steps - 1, phi_sib, half_sib, (k,))
         send[k] = acc[k].astype(BF16)
-        for copy in chip_copies(k):
+        for copy in first_copies(k):
             copy.start()
-        own[k] = acc[k, mine]
+
+    for k in range(BAND):
+        for copy in first_copies(k):
+            copy.wait_recv()
+        if k in X_FIRST:
+            away = acc[k, 1 - low, chip_x]
+            total = acc[k, low, chip_x]
+            for dx in range(3):
+                away = away + recv_x[k, dx, 1 - low].astype(F32)
+                total = total + recv_x[k, dx, low].astype(F32)
+            if k == 2:
+                mid_y32[...] = away
+            else:
+                mid_y[k] = away.astype(BF16)
+            if k == 0:
+                fin[...] = total
+            else:
+                own[k] = total
+        else:
+            acc[k, low] = acc[k, low] + recv_y[k].astype(F32)
+            mid_x[k] = acc[k, low].astype(BF16)
+            if k > 1:
+                own[k] = acc[k, low, chip_x]
+        for copy in second_copies(k):
+            copy.start()
 
     def collect(k):
-        for copy in chip_copies(k):
+        for copy in second_copies(k):
             copy.wait_recv()
+        if k == 0:
+            return fin_recv[...] + got_y[k].astype(F32)
+        if k == 1:
+            pieces = [got_x1[dx].astype(F32) for dx in range(X_CHIPS)]
+            return (pieces[0] + pieces[1]) + (pieces[2] + pieces[3])
         total = own[k]
-        for i in range(len(chips)):
-            total = total + recv[k, i].astype(F32)
+        if k == 2:
+            return total + got_y32[...]
+        if k in X_FIRST:
+            return total + got_y[k].astype(F32)
+        for dx in range(3):
+            total = total + got_x[k, dx].astype(F32)
         return total
 
-    last = [
-        remote(fin.at[0], fin_recv.at[0], f_send.at[0], f_recv.at[0], behind2),
-        remote(fin.at[1], fin_recv.at[1], f_send.at[1], f_recv.at[1], behind1),
-    ]
-    for k in range(2):
-        fin[k] = collect(k)
-        last[k].start()
-    totals = [collect(k) for k in (2, 3, 4)]
-    out[:, 0:rows] = totals[0]
+    out[:, 0:rows] = collect(2)
     for k in (1, 2):
-        last[2 - k].wait_recv()
-        out[:, k * rows : (k + 1) * rows] = totals[k] + fin_recv[2 - k]
+        ahead = collect(2 - k)
+        out[:, k * rows : (k + 1) * rows] = ahead + collect(k + 2)
 
     for j in range(steps):
         for copy in (*own_sends(j), *forwards(j)):
@@ -349,10 +398,8 @@
         for copy in (*a_copies(j), *b_copies(j), *sibling_blocks(j), sibling_half(j)):
             copy.wait_send()
     for k in range(BAND):
-        for copy in chip_copies(k):
+        for copy in first_copies(k) + second_copies(k):
             copy.wait_send()
-    for copy in last:
-        copy.wait_send()
 
 
 def body(basis_values, density, screen, atom_of_block, atom_factor, quad_weight, core_density):
@@ -377,22 +424,29 @@
             pltpu.VMEM((2 * rows, CHUNK), F32),
             pltpu.VMEM((steps, 8, CORES, piece, CHUNK), BF16),
             pltpu.VMEM((steps, 8, CORES, piece, CHUNK), BF16),
-            pltpu.VMEM((BAND, 8, piece, rows), F32),
+            pltpu.VMEM((BAND, Y_LOW, X_CHIPS, piece, rows), F32),
             pltpu.VMEM((steps, 4, flat, TILE), F32),
             pltpu.VMEM((steps, 3, flat, TILE), F32),
             pltpu.VMEM((steps, flat, TILE), F32),
             pltpu.VMEM((flat, TILE), F32),
-            pltpu.VMEM((BAND, 8, piece, rows), BF16),
+            pltpu.VMEM((BAND, Y_LOW, X_CHIPS, piece, rows), BF16),
+            pltpu.VMEM((BAND, X_CHIPS - 1, Y_LOW, piece, rows), BF16),
+            pltpu.VMEM((BAND, X_CHIPS, piece, rows), BF16),
+            pltpu.VMEM((BAND, piece, rows), BF16),
+            pltpu.VMEM((piece, rows), F32),
+            pltpu.VMEM((BAND, X_CHIPS, piece, rows), BF16),
+            pltpu.VMEM((BAND, piece, rows), BF16),
+            pltpu.VMEM((piece, rows), F32),
+            pltpu.VMEM((BAND, X_CHIPS - 1, piece, rows), BF16),
+            pltpu.VMEM((X_CHIPS, piece, rows), BF16),
             pltpu.VMEM((BAND, piece, rows), F32),
-            pltpu.VMEM((BAND, 7, piece, rows), BF16),
-            pltpu.VMEM((2, piece, rows), F32),
-            pltpu.VMEM((2, piece, rows), F32),
+            pltpu.VMEM((piece, rows), F32),
+            pltpu.VMEM((piece, rows), F32),
             dma((steps,)), dma((steps,)), dma,
             dma((4, 2, steps)), dma((4, 2, steps)),
             dma((steps, 3)), dma((steps, 3)), dma((steps, 3)), dma((steps, 3)),
             dma((3, steps)), dma((3, steps)),
-            dma((BAND, 7)), dma((BAND, 7)),
-            dma((2,)), dma((2,)),
+            dma((BAND, 3)), dma((BAND, 3)), dma((BAND, 4)), dma((BAND, 4)),
         ],
         compiler_params=pltpu.CompilerParams(
             collective_id=0, has_side_effects=True, vmem_limit_bytes=56 << 20

time: 83.4 us -> 81.3 us (0.975)
  Pallas kernels: 81.7 us -> 79 us
    pallas_call x1, Pallas kernels: 81.7 us -> 79 us  [body(): pl.pallas_call(kernel, out_shape=jax.ShapeDtypeStruct((piece, 3 * rows),...]
where the time goes in v3:
time: 81.3 us; the launch traced here: 80.6 us
  Pallas kernels  79 us (97%)
  local copies, waits for them, and re-layouts  1.62 us (2%)
    pallas_call x1, Pallas kernels, body(): pl.pallas_call(kernel, out_shape=jax.ShapeDtypeStruct((piece, 3 * rows),...  79 us

profile of v3, /device:TPU:1, one launch (start us, length us, event | category | flops | bytes accessed | tf_op | source)
XLA Modules:
  0.0 80.6 jit_solution(9539736755445562816)
XLA Ops:
  0.0 79.0 %xc_matrix.1 = f32[32,1536]{1,0:T(8,128)} custom-call(bf16[4,512,1024]{2,1,0:T(8,128)(2,1)} %basis.1, f32[512,2560]{1,0:T(8,128)} %dens.1, s32[4,8]{1,0:T(4,128)} %screen.1, s32[8]{0:T(128)} %atom.1, f32[64]{0:T(128)} %factor.1, f32[8,128]{1,0:T(8,128)} %bitcast.2, f32[8,128]{1,0:T(8,128)} %bitcast.3), custom_call_target="tpu_custom_call" | custom-call | tf_op jit(solution)/shard_map/xc_matrix/pallas_call | solution.py:412
  79.0 1.6 %copy.9 = f32[32,1536]{1,0:T(8,128)} copy(f32[32,1536]{1,0:T(8,128)} %xc_matrix.1) | data formatting | bytes 393216

commit v4 on v3

--- a/solution.py
+++ b/solution.py
@@ -105,7 +105,7 @@
         )
 
     def own_sends(j):
-        order = [(0, 0), (1, 1), (2, 0), (0, 1), (1, 0), (2, 1)]
+        order = [(0, 0), (2, 1), (0, 1), (1, 0), (1, 1), (2, 0)]
         place = [(2 - way, partner), (2 - 2 * way, far), (2 + 2 * way, near)]
         return [block_copy(j, route, 2, place[route][0], h, place[route][1]) for route, h in order]
 
@@ -345,6 +345,12 @@
         for copy in first_copies(k):
             copy.start()
 
+    for j in range(steps):
+        for copy in (*own_sends(j), *forwards(j)):
+            copy.wait_send()
+        for copy in (*a_copies(j), *b_copies(j), *sibling_blocks(j), sibling_half(j)):
+            copy.wait_send()
+
     for k in range(BAND):
         for copy in first_copies(k):
             copy.wait_recv()
@@ -392,11 +398,6 @@
         ahead = collect(2 - k)
         out[:, k * rows : (k + 1) * rows] = ahead + collect(k + 2)
 
-    for j in range(steps):
-        for copy in (*own_sends(j), *forwards(j)):
-            copy.wait_send()
-        for copy in (*a_copies(j), *b_copies(j), *sibling_blocks(j), sibling_half(j)):
-            copy.wait_send()
     for k in range(BAND):
         for copy in first_copies(k) + second_copies(k):
             copy.wait_send()

time: 81.3 us -> 81.1 us (level)
  no operation moved by 1% of the time
where the time goes in v4:
time: 81.1 us; the launch traced here: 80.5 us
  Pallas kernels  78.9 us (97%)
  local copies, waits for them, and re-layouts  1.62 us (2%)
    pallas_call x1, Pallas kernels, body(): pl.pallas_call(kernel, out_shape=jax.ShapeDtypeStruct((piece, 3 * rows),...  78.9 us

profile of v4, /device:TPU:1, one launch (start us, length us, event | category | flops | bytes accessed | tf_op | source)
XLA Modules:
  0.0 80.5 jit_solution(14355999378748363455)
XLA Ops:
  0.0 78.9 %xc_matrix.1 = f32[32,1536]{1,0:T(8,128)} custom-call(bf16[4,512,1024]{2,1,0:T(8,128)(2,1)} %basis.1, f32[512,2560]{1,0:T(8,128)} %dens.1, s32[4,8]{1,0:T(4,128)} %screen.1, s32[8]{0:T(128)} %atom.1, f32[64]{0:T(128)} %factor.1, f32[8,128]{1,0:T(8,128)} %bitcast.2, f32[8,128]{1,0:T(8,128)} %bitcast.3), custom_call_target="tpu_custom_call" | custom-call | tf_op jit(solution)/shard_map/xc_matrix/pallas_call | solution.py:413
  78.9 1.6 %copy.9 = f32[32,1536]{1,0:T(8,128)} copy(f32[32,1536]{1,0:T(8,128)} %xc_matrix.1) | data formatting | bytes 393216

commit v5 on v3

--- a/solution.py
+++ b/solution.py
@@ -339,13 +339,13 @@
 
     for copy in (*sibling_blocks(steps - 1), sibling_half(steps - 1)):
         copy.wait_recv()
-    for k in range(BAND):
+    for k in (2, 1, 0, 3, 4):
         matrix_part(steps - 1, phi_sib, half_sib, (k,))
         send[k] = acc[k].astype(BF16)
         for copy in first_copies(k):
             copy.start()
 
-    for k in range(BAND):
+    for k in (2, 1, 0, 3, 4):
         for copy in first_copies(k):
             copy.wait_recv()
         if k in X_FIRST:

time: 81.3 us -> 81.6 us (level)
  no operation moved by 1% of the time
where the time goes in v5:
time: 81.6 us; the launch traced here: 81.3 us
  Pallas kernels  79.7 us (98%)
  local copies, waits for them, and re-layouts  1.62 us (2%)
    pallas_call x1, Pallas kernels, body(): pl.pallas_call(kernel, out_shape=jax.ShapeDtypeStruct((piece, 3 * rows),...  79.7 us

profile of v5, /device:TPU:1, one launch (start us, length us, event | category | flops | bytes accessed | tf_op | source)
XLA Modules:
  0.0 81.3 jit_solution(12020903942107772426)
XLA Ops:
  0.0 79.7 %xc_matrix.1 = f32[32,1536]{1,0:T(8,128)} custom-call(bf16[4,512,1024]{2,1,0:T(8,128)(2,1)} %basis.1, f32[512,2560]{1,0:T(8,128)} %dens.1, s32[4,8]{1,0:T(4,128)} %screen.1, s32[8]{0:T(128)} %atom.1, f32[64]{0:T(128)} %factor.1, f32[8,128]{1,0:T(8,128)} %bitcast.2, f32[8,128]{1,0:T(8,128)} %bitcast.3), custom_call_target="tpu_custom_call" | custom-call | tf_op jit(solution)/shard_map/xc_matrix/pallas_call | solution.py:412
  79.7 1.6 %copy.9 = f32[32,1536]{1,0:T(8,128)} copy(f32[32,1536]{1,0:T(8,128)} %xc_matrix.1) | data formatting | bytes 393216
